TPU v7x, 32 devices: a whole 2x2x4 slice. The times are simulated.
32 devices in a mesh: seq: 4 (over z), exp: 8 (over y, x, core).
Axes of the slice: x: 2, y: 2, z: 4, core: 2. Of those that a mesh axis runs over, the one named last changes fastest.
Arguments:
- streams: bfloat16 [2048, 4, 3584], P(('seq', 'exp')), may hold values from -6 to 6
- phi_matrix: bfloat16 [24, 14336], replicated, may hold values from -0.046875 to 0.046875
- mix_scale: float32 [3], replicated, may hold values from 0.5 to 2
- mix_bias: float32 [24], replicated, may hold values from -1 to 1
- router: bfloat16 [32, 3584], replicated, may hold values from -0.09375 to 0.09375
- expert_index_table: int32 [2048, 8], P(('seq', 'exp')), may hold values from 0 to 31, all different within a row; in each aligned block of 64 rows (0 to 63, 64 to 127, ...) at most 20 rows name the same one
- w_gate: bfloat16 [32, 3584, 2048], P('exp', None, 'seq'), may hold values from -0.09375 to 0.09375
- w_up: bfloat16 [32, 3584, 2048], P('exp', None, 'seq'), may hold values from -0.09375 to 0.09375
- down_weight: bfloat16 [32, 2048, 3584], P('exp', 'seq'), may hold values from -0.125 to 0.125
Outputs:
- new_streams: bfloat16 [2048, 4, 3584], P(('seq', 'exp'))
Inputs may be any that keep to these rules, and one draw needn't show every extreme that they name: `expert_index_table`: each row names 8 different experts; among the 64 rows of one device (aligned blocks of 64 rows) no expert is named by more than 20 rows, a bound that some block reaches; every expert is named somewhere.
All inputs are finite; a program needn't handle non-finite values.
Results may differ from a plain program's by a relative error of at most 0.012.
Values may be sent and summed in bfloat16 or wider, within the bound.
A program may use at most 192 MiB of HBM per device.

v0:
```python
import jax
import jax.numpy as jnp
from jax import lax
from jax.sharding import PartitionSpec as P

BALANCE_SWEEPS = 20
EXPERTS = 32
CAP = 20


def mix_coefficients(streams, phi_matrix, mix_scale, mix_bias):
    count = streams.shape[1]
    flat = streams.astype(jnp.float32).reshape(streams.shape[0], -1)
    normed = flat * lax.rsqrt(jnp.mean(flat * flat, axis=1, keepdims=True) + 1e-06)
    normed = normed.astype(jnp.bfloat16)
    coeffs = lax.dot_general(
        normed, phi_matrix, (((1,), (1,)), ((), ())), preferred_element_type=jnp.float32
    )
    pre = jax.nn.sigmoid(mix_scale[0] * coeffs[:, :count] + mix_bias[:count])
    post = 2.0 * jax.nn.sigmoid(
        mix_scale[1] * coeffs[:, count : 2 * count] + mix_bias[count : 2 * count]
    )
    logits = mix_scale[2] * coeffs[:, 2 * count :] + mix_bias[2 * count :]
    mixing = jnp.exp(logits).reshape(-1, count, count)
    for sweep_step in range(BALANCE_SWEEPS):
        mixing = mixing / jnp.sum(mixing, axis=2, keepdims=True)
        mixing = mixing / jnp.sum(mixing, axis=1, keepdims=True)
    return (pre, post, mixing)


def mix_input(streams, pre):
    total = pre[:, 0, None] * streams[:, 0, :].astype(jnp.float32)
    for stream in range(1, streams.shape[1]):
        total = total + pre[:, stream, None] * streams[:, stream, :].astype(jnp.float32)
    return total.astype(jnp.bfloat16)


def mix_output(streams, mixing, post, moe_out):
    rows = []
    for target in range(streams.shape[1]):
        total = mixing[:, target, 0, None] * streams[:, 0, :].astype(jnp.float32)
        for source in range(1, streams.shape[1]):
            total = total + mixing[:, target, source, None] * streams[:, source, :].astype(
                jnp.float32
            )
        rows.append(total + post[:, target, None] * moe_out)
    return jnp.stack(rows, axis=1).astype(jnp.bfloat16)


def route_gates(layer_in, router, expert_index_table):
    logits = lax.dot_general(
        layer_in, router, (((1,), (1,)), ((), ())), preferred_element_type=jnp.float32
    )
    affinity = jax.nn.sigmoid(logits)
    chosen = jnp.take_along_axis(affinity, expert_index_table, axis=1)
    return 2.5 * chosen / jnp.sum(chosen, axis=1, keepdims=True)


def slot_ranks(expert_index_table):
    flat = expert_index_table.reshape(-1)
    onehot = (flat[:, None] == lax.iota(jnp.int32, EXPERTS)[None, :]).astype(jnp.int32)
    prior_value = jnp.cumsum(onehot, axis=0) - onehot
    return jnp.sum(prior_value * onehot, axis=1).reshape(expert_index_table.shape)


def expert_block(blocks, w_gate, w_up, down_weight):
    count, local, slots, width = blocks.shape
    rows = blocks.transpose(1, 0, 2, 3).reshape(local, count * slots, width)
    gate_part = jnp.einsum("erd,edf->erf", rows, w_gate, preferred_element_type=jnp.float32)
    up_part = jnp.einsum("erd,edf->erf", rows, w_up, preferred_element_type=jnp.float32)
    hidden = (jax.nn.silu(gate_part) * up_part).astype(jnp.bfloat16)
    part = jnp.einsum(
        "erf,efd->erd", hidden, down_weight, preferred_element_type=jnp.float32
    ).astype(jnp.bfloat16)
    return part.reshape(local, count, slots, width).transpose(1, 0, 2, 3)


def weigh_slots(returned_rows, targets, gates):
    selected_slot = jnp.take(returned_rows, targets.reshape(-1), axis=0).astype(jnp.float32)
    selected_slot = selected_slot.reshape(
        targets.shape[0], targets.shape[1], returned_rows.shape[1]
    )
    return jnp.sum(gates[:, :, None] * selected_slot, axis=1)


def body(
    streams, phi_matrix, mix_scale, mix_bias, router, expert_index_table, w_gate, w_up, down_weight
):
    pre, post, mixing = mix_coefficients(streams, phi_matrix, mix_scale, mix_bias)
    layer_in = mix_input(streams, pre)
    width = layer_in.shape[1]
    owners = lax.axis_size("exp")
    local = w_gate.shape[0]
    column_in, column_ids = (
        lax.all_gather(layer_in, "seq", axis=0, tiled=True),
        lax.all_gather(expert_index_table, "seq", axis=0, tiled=True),
    )
    sources = lax.axis_size("seq")
    tok_count = layer_in.shape[0]
    topk = expert_index_table.shape[1]
    gates = route_gates(column_in, router, column_ids)
    ranks = jax.vmap(slot_ranks)(column_ids.reshape(sources, tok_count, topk)).reshape(
        column_ids.shape
    )
    source_lookup = (lax.iota(jnp.int32, sources * tok_count) // tok_count)[:, None]
    targets = (column_ids * sources + source_lookup) * CAP + ranks
    places = lax.iota(jnp.int32, EXPERTS * sources * CAP)
    dispatch = jnp.any(places[:, None, None] == targets[None, :, :], axis=2).astype(jnp.bfloat16)
    send = jnp.dot(dispatch, column_in, preferred_element_type=jnp.float32).astype(jnp.bfloat16)
    send = send.reshape(owners, local, sources * CAP, width)
    part = expert_block(
        lax.all_to_all(send, "exp", split_axis=0, concat_axis=0, tiled=True),
        w_gate,
        w_up,
        down_weight,
    )
    returned = lax.all_to_all(part, "exp", split_axis=0, concat_axis=0, tiled=True)
    weighted = weigh_slots(returned.reshape(-1, width), targets, gates)
    moe_out = lax.psum_scatter(
        weighted.astype(jnp.bfloat16), "seq", scatter_dimension=0, tiled=True
    ).astype(jnp.float32)
    return mix_output(streams, mixing, post, moe_out)


def solution(mesh):
    in_specs = (
        P(("seq", "exp"), None, None),
        P(),
        P(),
        P(),
        P(),
        P(("seq", "exp"), None),
        P("exp", None, "seq"),
        P("exp", None, "seq"),
        P("exp", "seq", None),
    )
    out_specs = P(("seq", "exp"), None, None)
    return jax.shard_map(body, mesh=mesh, in_specs=in_specs, out_specs=out_specs, check_vma=False)
```

profile of v0, /device:TPU:0, one launch (start us, length us, event | category | flops | bytes accessed | tf_op | source)
XLA Modules:
  0.0 671.5 jit_solution(7974896404018500860)
XLA Ops:
  6.6 3.1 multiply_reduce_fusion.1
  9.7 7.0 %fusion.111 = (bf16[64,1,3584]{2,1,0:T(2,128)(2,1)S(1)}, bf16[64,1,3584]{2,1,0:T(2,128)(2,1)S(1)}, bf16[64,1,3584]{2,1,0:T(2,128)(2,1)S(1)}, bf16[64,1,3584]{2,1,0:T(2,128)(2,1)S(1)}) fusion(bf16[64,4,3584]{2,1,0:T(4,128)(2,1)} %param.9), kind=kLoop, calls=%fused_computation.238 | loop fusion | bytes 3670016 | tf_op jit(solution)/shard_map/slice | solution.py:41
  18.6 2.0 fusion.89
  20.6 1.7 fusion.59
  22.4 14.9 %all-gather = s32[4,64,8]{1,2,0:T(8,128)S(1)} all-gather(s32[1,64,8]{1,2,0:T(8,128)S(1)} %bitcast.166), channel_id=1, replica_groups=mesh['seq'=4,'exp'=8] {'seq'}, dimensions={0}, use_global_device_ids=true | all-gather | bytes 10240 | tf_op jit(solution)/shard_map/all_gather | solution.py:96
  37.7 4.6 reduce-window.6
  43.3 13.7 %fusion.19 = pred[2560,256]{1,0:T(8,128)(4,1)S(1)} fusion(s32[256,8]{0,1:T(8,128)S(1)} %get-tuple-element.6), kind=kLoop, calls=%fused_computation.24 | loop fusion | flops 9830400 | bytes 663552 | tf_op jit(solution)/shard_map/reduce_or | solution.py:108
  56.9 9.7 %all-gather.3.cloned.1.call-done = bf16[256,3584]{1,0:T(8,128)(2,1)} async-done(((bf16[64,3584]{1,0:T(8,128)(2,1)}), bf16[256,3584]{1,0:T(8,128)(2,1)}) %all-gather.3.cloned.1.call-update) | async-done | bytes 1835024 | tf_op jit(solution)/shard_map/all_gather | solution.py:95
  66.7 10.3 %convolution_convert_fusion = bf16[2560,3584]{1,0:T(8,128)(2,1)} fusion(pred[2560,256]{1,0:T(8,128)(4,1)S(1)} %fusion.19, bf16[256,3584]{1,0:T(8,128)(2,1)} %all-gather.3.cloned.1.call-done), kind=kOutput, calls=%fused_computation.22 | convolution fusion | flops 4706795520 | bytes 20840448 | tf_op jit(solution)/shard_map/dot_general | solution.py:109
  77.0 205.0 %all_to_all.10 = bf16[8,4,80,3584]{3,2,1,0:T(8,128)(2,1)S(1)} all-to-all(bf16[8,4,80,3584]{3,2,1,0:T(8,128)(2,1)} %bitcast.133), channel_id=1, replica_groups=mesh['seq'=4,'exp'=8] {'exp'}, dimensions={0} | all-to-all | bytes 36700160 | tf_op jit(solution)/shard_map/all_to_all | solution.py:112
  281.9 6.5 copy.68
  288.4 19.1 %fusion.115 = f32[4,640,512]{2,1,0:T(8,128)} fusion(bf16[4,640,3584]{2,1,0:T(8,128)(2,1)} %bitcast.136, bf16[4,3584,512]{2,1,0:T(8,128)(2,1)} %param.16), kind=kOutput, calls=%fused_computation.242 | convolution fusion | flops 9395240960 | bytes 38273024 | tf_op jit(solution)/shard_map/erd,edf->erf/dot_general | solution.py:70
  307.5 19.1 %fusion.114 = f32[4,640,512]{2,1,0:T(8,128)} fusion(bf16[4,640,3584]{2,1,0:T(8,128)(2,1)} %bitcast.137, bf16[4,3584,512]{2,1,0:T(8,128)(2,1)} %param.15), kind=kOutput, calls=%fused_computation.241 | convolution fusion | flops 9395240960 | bytes 38273024 | tf_op jit(solution)/shard_map/erd,edf->erf/dot_general | solution.py:69
  326.6 19.9 %convolution_convert_fusion.1 = bf16[4,640,3584]{2,1,0:T(8,128)(2,1)} fusion(bf16[4,512,3584]{2,1,0:T(8,128)(2,1)} %param.17, f32[4,640,512]{2,1,0:T(8,128)} %fusion.115, f32[4,640,512]{2,1,0:T(8,128)} %fusion.114), kind=kOutput, calls=%fused_computation.27 | convolution fusion | flops 9412280320 | bytes 43515904 | tf_op jit(solution)/shard_map/erf,efd->erd/dot_general | solution.py:72
  346.5 15.6 %copy.88 = bf16[4,8,80,3584]{3,2,0,1:T(8,128)(2,1)} copy(bf16[4,8,80,3584]{3,2,1,0:T(8,128)(2,1)} %bitcast.138) | data formatting | bytes 36700160 | tf_op jit(solution)/shard_map/reshape | solution.py:75
  362.2 6.0 all-to-all-start.1
  370.5 17.0 %gather_fusion.1 = f32[2048]{0:T(1024)S(1)} fusion(f32[256,32]{0,1:T(8,128)S(1)} %fusion.25, s32[2048]{0:T(1024)S(1)} %reshape.208), kind=kCustom, calls=%fused_computation.1 | custom fusion | bytes 32768 | tf_op jit(solution)/shard_map/jit(take_along_axis)/gather | solution.py:55
  387.9 181.1 %all-to-all-done.1 = bf16[8,4,80,3584]{3,2,1,0:T(8,128)(2,1)} async-done(((bf16[8,4,80,3584]{3,2,1,0:T(8,128)(2,1)}), bf16[8,4,80,3584]{3,2,1,0:T(8,128)(2,1)}, u32[]{:S(2)}, u32[]{:S(2)}) %all-to-all-start.1) | async-done | bytes 18350112 | tf_op jit(solution)/shard_map/all_to_all | solution.py:117
  569.0 34.7 %gather_fusion = bf16[2048,3584]{1,0:T(8,128)(2,1)} fusion(bf16[2560,3584]{1,0:T(8,128)(2,1)} %bitcast.29, s32[2048]{0:T(1024)S(1)} %broadcast_clamp_fusion), kind=kCustom, calls=%fused_computation | custom fusion | bytes 29368320 | tf_op jit(solution)/shard_map/jit(_take)/gather | solution.py:79
  603.7 17.4 %multiply_reduce_fusion = bf16[256,3584]{1,0:T(8,128)(2,1)} fusion(bf16[2048,3584]{1,0:T(8,128)(2,1)} %gather_fusion, f32[256,8]{1,0:T(8,128)S(1)} %copy.62, pred[256,8]{1,0:T(8,128)(4,1)S(1)} %copy.67), kind=kLoop, calls=%fused_computation.21 | loop fusion | flops 28442624 | bytes 16525312 | tf_op jit(solution)/shard_map/reduce_sum | solution.py:83
  621.7 36.2 %reduce-scatter.2.cloned.1.call-done = bf16[64,3584]{1,0:T(8,128)(2,1)} async-done(((bf16[256,3584]{1,0:T(8,128)(2,1)}), bf16[64,3584]{1,0:T(8,128)(2,1)}) %reduce-scatter.2.cloned.1.call-update) | async-done | bytes 458768 | tf_op jit(solution)/shard_map/reduce_scatter | solution.py:119
  657.8 1.9 fusion.70
  659.8 2.0 fusion.72
  662.0 2.6 copy.71
  (92 shorter events, 6.7 us)
Async XLA Ops:
  6.5 11.4 %copy-start = (bf16[24,14336]{1,0:T(8,128)(2,1)S(1)}, bf16[24,14336]{1,0:T(8,128)(2,1)}, u32[]{:S(2)}) copy-start(bf16[24,14336]{1,0:T(8,128)(2,1)} %param.10) | copy-start | bytes 2064388
  6.5 10.9 %copy-start.2 = (bf16[64,4,3584]{2,1,0:T(4,128)(2,1)S(1)}, bf16[64,4,3584]{2,1,0:T(4,128)(2,1)}, u32[]{:S(2)}) copy-start(bf16[64,4,3584]{2,1,0:T(4,128)(2,1)} %param.9) | copy-start | bytes 5505028
  6.5 10.2 %copy-start.12 = (f32[24]{0:T(128)S(1)}, f32[24]{0:T(128)}, u32[]{:S(2)}) copy-start(f32[24]{0:T(128)} %param.12) | copy-start | bytes 292
  6.5 10.2 %copy-start.10 = (f32[3]{0:T(128)S(1)}, f32[3]{0:T(128)}, u32[]{:S(2)}) copy-start(f32[3]{0:T(128)} %param.11) | copy-start | bytes 40
  6.5 60.1 %all-gather.3.cloned.1.call-start = ((), (), s32[]{:S(2)}) async-start(), calls=%async_computation.3 | async-start | bytes 2293760 | tf_op jit(solution)/shard_map/all_gather | solution.py:95
  17.9 4.4 copy-start.11
  362.2 7.7 %copy-start.3 = (bf16[256,3584]{1,0:T(8,128)(2,1)S(1)}, bf16[256,3584]{1,0:T(8,128)(2,1)}, u32[]{:S(2)}) copy-start(bf16[256,3584]{1,0:T(8,128)(2,1)} %all-gather.3.cloned.1.call-done) | copy-start | bytes 5505028
  362.2 7.7 %copy-start.8 = (bf16[32,3584]{1,0:T(8,128)(2,1)S(1)}, bf16[32,3584]{1,0:T(8,128)(2,1)}, u32[]{:S(2)}) copy-start(bf16[32,3584]{1,0:T(8,128)(2,1)} %param.13) | copy-start | bytes 688132
  362.2 206.8 %all-to-all-start.1 = ((bf16[8,4,80,3584]{3,2,1,0:T(8,128)(2,1)}), bf16[8,4,80,3584]{3,2,1,0:T(8,128)(2,1)}, u32[]{:S(2)}, u32[]{:S(2)}) async-start(bf16[8,4,80,3584]{3,2,1,0:T(8,128)(2,1)} %bitcast.132), calls=%async_computation.1 | async-start | bytes 36700160 | tf_op jit(solution)/shard_map/all_to_all | solution.py:117
  368.2 289.7 %reduce-scatter.2.cloned.1.call-start = ((), (), s32[]{:S(2)}) async-start(), calls=%async_computation.4 | async-start | bytes 2293760 | tf_op jit(solution)/shard_map/reduce_scatter | solution.py:119
  603.6 17.4 %copy-start.9 = (f32[64,4]{0,1:T(4,128)S(1)}, f32[64,4]{0,1:T(4,128)}, u32[]{:S(2)}) copy-start(f32[64,4]{0,1:T(4,128)} %get-tuple-element.20) | copy-start | bytes 3076
  603.6 54.2 %copy-start.4 = (bf16[64,3584]{1,0:T(8,128)(2,1)S(1)}, bf16[64,3584]{1,0:T(8,128)(2,1)}, u32[]{:S(2)}) copy-start(bf16[64,3584]{1,0:T(8,128)(2,1)} %get-tuple-element.8) | copy-start | bytes 1376260
  603.6 54.2 %copy-start.5 = (bf16[64,3584]{1,0:T(8,128)(2,1)S(1)}, bf16[64,3584]{1,0:T(8,128)(2,1)}, u32[]{:S(2)}) copy-start(bf16[64,3584]{1,0:T(8,128)(2,1)} %get-tuple-element.9) | copy-start | bytes 1376260
  603.6 54.2 %copy-start.6 = (bf16[64,3584]{1,0:T(8,128)(2,1)S(1)}, bf16[64,3584]{1,0:T(8,128)(2,1)}, u32[]{:S(2)}) copy-start(bf16[64,3584]{1,0:T(8,128)(2,1)} %get-tuple-element.10) | copy-start | bytes 1376260
  603.7 54.2 %copy-start.7 = (bf16[64,3584]{1,0:T(8,128)(2,1)S(1)}, bf16[64,3584]{1,0:T(8,128)(2,1)}, u32[]{:S(2)}) copy-start(bf16[64,3584]{1,0:T(8,128)(2,1)} %get-tuple-element.11) | copy-start | bytes 1376260
  659.8 4.9 copy-start.1
Sparse Core Ops, SparseCore 0:
  22.5 44.1 all-gather.2
  621.2 36.6 reduce-scatter.1
where the time goes:
time: 672 us; the launch traced here: 671 us
  waiting for transfers between devices  227 us (34%)
  blocking collectives  220 us (33%)
  local copies, waits for them, and re-layouts  86.8 us (13%)
  matrix products  69.7 us (10%)
  other arithmetic  48.3 us (7%)
  between operations  13.8 us (2%)
    all_to_all x1, blocking collectives, body(): lax.all_to_all(send, 'exp', split_axis=0, concat_axis=0, tiled=True)  205 us
    all_to_all x1, waiting for transfers between devices, body(): lax.all_to_all(part, 'exp', split_axis=0, concat_axis=0, tiled=True)  181 us
    reduce_scatter x1, waiting for transfers between devices, body(): lax.psum_scatter(weighted.astype(jnp.bfloat16), 'seq', scatter_dimension=...  36.2 us
    gather x1, local copies, waits for them, and re-layouts, weigh_slots(): jnp.take(returned_rows, targets.reshape(-1), axis=0).astype(jnp.float32)  34.7 us
    dot_general x1, matrix products, expert_block(): jnp.einsum('erf,efd->erd', hidden, down_weight, preferred_element_type=jn...  19.9 us
    dot_general x1, matrix products, expert_block(): jnp.einsum('erd,edf->erf', rows, w_gate, preferred_element_type=jnp.float32)  19.1 us
    dot_general x1, matrix products, expert_block(): jnp.einsum('erd,edf->erf', rows, w_up, preferred_element_type=jnp.float32)  19.1 us
    gather x5, local copies, waits for them, and re-layouts, route_gates(): chosen = jnp.take_along_axis(affinity, expert_index_table, axis=1)  17.4 us
  transfers between devices with their start and end apart: 3, of which 3 were waited for; matrix products, arithmetic and copies ran while one was open for 6% of the time, Pallas kernels for 0%

commit v1 on v0

--- a/solution.py
+++ b/solution.py
@@ -1,11 +1,16 @@
+import functools
+
 import jax
 import jax.numpy as jnp
 from jax import lax
+from jax.experimental import pallas as pl
+from jax.experimental.pallas import tpu as pltpu
 from jax.sharding import PartitionSpec as P
 
 BALANCE_SWEEPS = 20
 EXPERTS = 32
 CAP = 20
+MESH = pl.DeviceIdType.MESH
 
 
 def mix_coefficients(streams, phi_matrix, mix_scale, mix_bias):
@@ -122,6 +127,389 @@
     return mix_output(streams, mixing, post, moe_out)
 
 
+def swap(exp, bit):
+    side = lax.rem(exp // bit, 2)
+    return exp + bit - 2 * bit * side
+
+
+def greet(peers):
+    barrier = pltpu.get_barrier_semaphore()
+    for peer in peers:
+        pl.semaphore_signal(barrier, inc=1, device_id=peer, device_id_type=MESH)
+    pl.semaphore_wait(barrier, len(peers))
+
+
+def place(planes, exps):
+    z, e = lax.axis_index("seq"), lax.axis_index("exp")
+    core, x, y = swap(e, 1), swap(e, 2), swap(e, 4)
+    both = swap(x, 4)
+    return z, e, core, x, y, both
+
+
+def gather_kernel(planes, exps, block, out, s_z, r_z, s_1, r_1, s_2, r_2, s_c, r_c, s_own):
+    z, e, core, x, y, both = place(planes, exps)
+    half_rows = block.shape[0] // 2
+    first, second = (x, y), (y, x)
+    greet([(lax.rem(z + d, planes), e) for d in range(1, planes)] + [(z, x), (z, y), (z, core)])
+    started = []
+
+    def rows(half):
+        return pl.ds(half * half_rows, half_rows)
+
+    def push(src, plane, exp, half, send, recv, target):
+        copy = pltpu.make_async_remote_copy(
+            src_ref=src,
+            dst_ref=out.at[plane * exps + exp, rows(half)],
+            send_sem=send,
+            recv_sem=recv,
+            device_id=target,
+            device_id_type=MESH,
+        )
+        copy.start()
+        started.append(copy)
+
+    def arrive(plane, exp, half, sem):
+        spot = out.at[plane * exps + exp, rows(half)]
+        pltpu.make_async_copy(spot, spot, sem).wait()
+
+    def plane_at(k):
+        return lax.rem(z + planes - k, planes)
+
+    def local(k, exp, half):
+        if k == 0 and exp is e:
+            return block.at[rows(half)]
+        return out.at[plane_at(k) * exps + exp, rows(half)]
+
+    def across(k, exp, half, index):
+        push(local(k, exp, half), plane_at(k), exp, half, s_c.at[k, half, index], r_c.at[k, half, index], (z, core))
+
+    def spread_own(k):
+        for half in (0, 1):
+            if k:
+                arrive(plane_at(k), e, half, r_z.at[k - 1, half])
+            push(local(k, e, half), plane_at(k), e, half, s_1.at[k, half], r_1.at[k, half], (z, first[half]))
+            push(local(k, e, half), plane_at(k), e, half, s_2.at[k, half, 0], r_2.at[k, half, 0], (z, second[half]))
+            across(k, e, half, 0)
+
+    def spread_first(k):
+        for half in (0, 1):
+            arrive(plane_at(k), first[half], half, r_1.at[k, half])
+            push(local(k, first[half], half), plane_at(k), first[half], half, s_2.at[k, half, 1], r_2.at[k, half, 1], (z, second[half]))
+            across(k, first[half], half, 1)
+
+    def spread_second(k):
+        for half in (0, 1):
+            for index, exp in enumerate((second[half], both)):
+                arrive(plane_at(k), exp, half, r_2.at[k, half, index])
+                across(k, exp, half, 2 + index)
+
+    own = pltpu.make_async_copy(block, out.at[z * exps + e], s_own)
+    own.start()
+    for d in range(1, planes):
+        for half in (0, 1):
+            push(block.at[rows(half)], z, e, half, s_z.at[d - 1, half], r_z.at[d - 1, half], (lax.rem(z + d, planes), e))
+    spread_own(0)
+    for k in range(1, planes + 2):
+        if k < planes:
+            spread_own(k)
+        if k - 1 < planes:
+            spread_first(k - 1)
+        if k >= 2:
+            spread_second(k - 2)
+    for k in range(planes):
+        for half in (0, 1):
+            here = (core, swap(first[half], 1), swap(second[half], 1), swap(both, 1))
+            for index, exp in enumerate(here):
+                arrive(plane_at(k), exp, half, r_c.at[k, half, index])
+    for copy in started:
+        copy.wait_send()
+    own.wait()
+
+
+def gather_tokens(block, planes, exps):
+    dma = pltpu.SemaphoreType.DMA
+    shapes = [(planes - 1, 2), (planes, 2), (planes, 2, 2), (planes, 2, 4)]
+    return pl.pallas_call(
+        functools.partial(gather_kernel, planes, exps),
+        out_shape=jax.ShapeDtypeStruct((planes * exps,) + block.shape, block.dtype),
+        in_specs=[pl.BlockSpec(memory_space=pl.ANY)],
+        out_specs=pl.BlockSpec(memory_space=pl.ANY),
+        scratch_shapes=[dma(shape) for shape in shapes for way in range(2)] + [dma],
+        compiler_params=pltpu.CompilerParams(collective_id=0, has_side_effects=True),
+        name="gather_tokens",
+    )(block)
+
+
+def scatter_kernel(planes, exps, parts, out, held, in_c, in_2, in_1, in_z,
+                   s_own, s_c, r_c, s_2, r_2, s_1, r_1, s_z, r_z):
+    z, e, core, x, y, both = place(planes, exps)
+    tokens, width = out.shape
+    half_rows = tokens // 2
+    step = 512 if width % 512 == 0 else width
+    first, second = (x, y), (y, x)
+    greet([(lax.rem(z + d, planes), e) for d in range(1, planes)] + [(z, x), (z, y), (z, core)])
+    started = []
+
+    def rows(half):
+        return pl.ds(half * half_rows, half_rows)
+
+    def push(src, dst, send, recv, target):
+        copy = pltpu.make_async_remote_copy(
+            src_ref=src, dst_ref=dst, send_sem=send, recv_sem=recv, device_id=target, device_id_type=MESH
+        )
+        copy.start()
+        started.append(copy)
+
+    def arrive(spot, sem):
+        pltpu.make_async_copy(spot, spot, sem).wait()
+
+    def add(total, term):
+        def one(i, carry):
+            columns = pl.ds(pl.multiple_of(i * step, step), step)
+            total[:, columns] = (
+                total[:, columns].astype(jnp.float32) + term[:, columns].astype(jnp.float32)
+            ).astype(total.dtype)
+            return carry
+
+        lax.fori_loop(0, width // step, one, 0)
+
+    def plane_at(k):
+        return lax.rem(z + k, planes)
+
+    def dests(half):
+        return (both, second[half], first[half], e)
+
+    order = [k for k in range(1, planes)] + [0]
+    loads = {}
+    for k in order:
+        for half in (0, 1):
+            for index, exp in enumerate(dests(half)):
+                away = parts.at[plane_at(k) * exps + swap(exp, 1), rows(half)]
+                push(away, in_c.at[k, half, index], s_c.at[k, half, index], r_c.at[k, half, index], (z, core))
+                load = pltpu.make_async_copy(
+                    parts.at[plane_at(k) * exps + exp, rows(half)], held.at[k, half, index], s_own.at[k, half, index]
+                )
+                load.start()
+                loads[k, half, index] = load
+
+    def merge_core(k):
+        for half in (0, 1):
+            for index in range(4):
+                loads[k, half, index].wait()
+                arrive(in_c.at[k, half, index], r_c.at[k, half, index])
+                add(held.at[k, half, index], in_c.at[k, half, index])
+                if index < 2:
+                    push(held.at[k, half, index], in_2.at[k, half, index], s_2.at[k, half, index], r_2.at[k, half, index], (z, second[half]))
+
+    def merge_second(k):
+        for half in (0, 1):
+            for index in (0, 1):
+                arrive(in_2.at[k, half, index], r_2.at[k, half, index])
+                add(held.at[k, half, 2 + index], in_2.at[k, half, index])
+                if index == 0:
+                    push(held.at[k, half, 2], in_1.at[k, half], s_1.at[k, half], r_1.at[k, half], (z, first[half]))
+
+    def merge_first(k):
+        for half in (0, 1):
+            arrive(in_1.at[k, half], r_1.at[k, half])
+            add(held.at[k, half, 3], in_1.at[k, half])
+            if k:
+                push(held.at[k, half, 3], in_z.at[k - 1, half], s_z.at[k - 1, half], r_z.at[k - 1, half], (plane_at(k), e))
+
+    for turn in range(planes + 2):
+        if turn < planes:
+            merge_core(order[turn])
+        if 1 <= turn <= planes:
+            merge_second(order[turn - 1])
+        if turn >= 2:
+            merge_first(order[turn - 2])
+    for k in range(1, planes):
+        for half in (0, 1):
+            arrive(in_z.at[k - 1, half], r_z.at[k - 1, half])
+    for half in (0, 1):
+        def one(i, carry):
+            columns = pl.ds(pl.multiple_of(i * step, step), step)
+            total = held[0, half, 3, :, columns].astype(jnp.float32)
+            for k in range(1, planes):
+                total = total + in_z[k - 1, half, :, columns].astype(jnp.float32)
+            out[half * half_rows : (half + 1) * half_rows, columns] = total
+            return carry
+
+        lax.fori_loop(0, width // step, one, 0)
+    for copy in started:
+        copy.wait_send()
+
+
+def scatter_sum(parts, planes, exps):
+    blocks, tokens, width = parts.shape
+    dma = pltpu.SemaphoreType.DMA
+    half = (tokens // 2, width)
+    shapes = [(planes, 2, 4), (planes, 2, 2), (planes, 2), (planes - 1, 2)]
+    return pl.pallas_call(
+        functools.partial(scatter_kernel, planes, exps),
+        out_shape=jax.ShapeDtypeStruct((tokens, width), jnp.float32),
+        in_specs=[pl.BlockSpec(memory_space=pl.ANY)],
+        out_specs=pl.BlockSpec(memory_space=pltpu.VMEM),
+        scratch_shapes=[pltpu.VMEM(shape + half, parts.dtype) for shape in [shapes[0]] + shapes]
+        + [dma(shapes[0])]
+        + [dma(shape) for shape in shapes for way in range(2)],
+        compiler_params=pltpu.CompilerParams(
+            collective_id=1, has_side_effects=True, vmem_limit_bytes=48 * 1024 * 1024
+        ),
+        name="scatter_sum",
+    )(parts)
+
+
+def expert_kernel(tokens, spread, collect, slot_gates, w_gate, w_up, w_down, out,
+                  held, slots, hidden, in_sems, out_sems):
+    groups, group_rows, width = held.shape
+    own = pl.program_id(0)
+    last = pl.num_programs(0) - 1
+    room = slots.shape[1] // pl.num_programs(0)
+    ff = hidden.shape[1]
+    wide = 896 if width % 896 == 0 else width
+    tall = 256 if ff % 256 == 0 else ff
+
+    def load(g):
+        return pltpu.make_async_copy(tokens.at[g, :, pl.ds(0, width)], held.at[g], in_sems.at[g])
+
+    def store(g):
+        return pltpu.make_async_copy(held.at[g], out.at[g], out_sems.at[g])
+
+    @pl.when(own == 0)
+    def dispatch():
+        for g in range(groups):
+            load(g).start()
+        for g in range(groups):
+            load(g).wait()
+
+            def one(i, carry):
+                columns = pl.ds(pl.multiple_of(i * wide, wide), wide)
+                slots[g, :, columns] = jnp.dot(
+                    spread[g], held[g, :, columns], preferred_element_type=jnp.float32
+                ).astype(slots.dtype)
+                return carry
+
+            lax.fori_loop(0, width // wide, one, 0)
+
+    mine = pl.ds(pl.multiple_of(own * room, room), room)
+    for i in range(ff // tall):
+        columns = pl.ds(i * tall, tall)
+        rows = slots[:, mine, :].reshape(groups * room, width)
+        gate_part = jnp.dot(rows, w_gate[0, :, columns], preferred_element_type=jnp.float32)
+        up_part = jnp.dot(rows, w_up[0, :, columns], preferred_element_type=jnp.float32)
+        hidden[:, columns] = (
+            gate_part / (1.0 + jnp.exp(-gate_part)) * up_part * slot_gates[0]
+        ).astype(hidden.dtype)
+
+    def down(i, carry):
+        columns = pl.ds(pl.multiple_of(i * wide, wide), wide)
+        part = jnp.dot(hidden[...], w_down[0, :, columns], preferred_element_type=jnp.float32)
+        slots[:, mine, columns] = part.astype(slots.dtype).reshape(groups, room, wide)
+        return carry
+
+    lax.fori_loop(0, width // wide, down, 0)
+
+    @pl.when(own == last)
+    def combine():
+        for g in range(groups):
+
+            def one(i, carry):
+                columns = pl.ds(pl.multiple_of(i * wide, wide), wide)
+                held[g, :, columns] = jnp.dot(
+                    collect[g], slots[g, :, columns], preferred_element_type=jnp.float32
+                ).astype(held.dtype)
+                return carry
+
+            lax.fori_loop(0, width // wide, one, 0)
+            store(g).start()
+        for g in range(groups):
+            store(g).wait()
+
+
+def run_experts(tokens, spread, slot_gates, w_gate, w_up, down_weight):
+    groups, rows, _ = tokens.shape
+    local, width, ff = w_gate.shape
+    room = spread.shape[1] // local
+    collect = spread.transpose(0, 2, 1)
+
+    def whole(array):
+        return pl.BlockSpec(array.shape, lambda i: (0,) * array.ndim, pipeline_mode=pl.Buffered(1))
+
+    def each(array):
+        return pl.BlockSpec((1,) + array.shape[1:], lambda i: (i, 0, 0))
+
+    return pl.pallas_call(
+        expert_kernel,
+        grid=(local,),
+        out_shape=jax.ShapeDtypeStruct((groups, rows, width), jnp.bfloat16),
+        in_specs=[pl.BlockSpec(memory_space=pl.ANY), whole(spread), whole(collect)]
+        + [each(a) for a in (slot_gates, w_gate, w_up, down_weight)],
+        out_specs=pl.BlockSpec(memory_space=pl.ANY),
+        scratch_shapes=[
+            pltpu.VMEM((groups, rows, width), jnp.bfloat16),
+            pltpu.VMEM((groups, local * room, width), jnp.bfloat16),
+            pltpu.VMEM((groups * room, ff), jnp.bfloat16),
+            pltpu.SemaphoreType.DMA((groups,)),
+            pltpu.SemaphoreType.DMA((groups,)),
+        ],
+        compiler_params=pltpu.CompilerParams(
+            dimension_semantics=("arbitrary",), vmem_limit_bytes=64 * 1024 * 1024 - 128 * 1024
+        ),
+        name="run_experts",
+    )(tokens, spread, collect, slot_gates, w_gate, w_up, down_weight)
+
+
+def dense_gates(layer_in, router, expert_index_table):
+    logits = lax.dot_general(
+        layer_in, router, (((1,), (1,)), ((), ())), preferred_element_type=jnp.float32
+    )
+    names = lax.iota(jnp.int32, EXPERTS)
+    hits = jnp.any(expert_index_table[:, :, None] == names[None, None, :], axis=1)
+    chosen = jnp.where(hits, jax.nn.sigmoid(logits), 0.0)
+    return 2.5 * chosen / jnp.sum(chosen, axis=1, keepdims=True)
+
+
+def fast_body(
+    streams, phi_matrix, mix_scale, mix_bias, router, expert_index_table, w_gate, w_up, down_weight
+):
+    planes, exps = lax.axis_size("seq"), lax.axis_size("exp")
+    pre, post, mixing = mix_coefficients(streams, phi_matrix, mix_scale, mix_bias)
+    layer_in = mix_input(streams, pre)
+    count, width = layer_in.shape
+    local = w_gate.shape[0]
+    gates = dense_gates(layer_in, router, expert_index_table)
+    high = gates.astype(jnp.bfloat16)
+    low = (gates - high.astype(jnp.float32)).astype(jnp.bfloat16)
+    filler = jnp.zeros((count, 128 - 2 * EXPERTS), jnp.bfloat16)
+    block = jnp.concatenate([layer_in, high, low, filler], axis=1)
+    everyone = gather_tokens(block, planes, exps)
+    owner = lax.axis_index("exp")
+    tail = everyone[:, :, width:].astype(jnp.float32)
+    tail = tail[:, :, :EXPERTS] + tail[:, :, EXPERTS : 2 * EXPERTS]
+    mine = lax.dynamic_slice_in_dim(tail, owner * local, local, axis=2)
+    mine = mine.transpose(0, 2, 1)
+    taken = mine > 0
+    before = (lax.iota(jnp.int32, count)[:, None] < lax.iota(jnp.int32, count)[None, :]).astype(jnp.bfloat16)
+    ranks = jnp.dot(taken.astype(jnp.bfloat16).reshape(-1, count), before, preferred_element_type=jnp.float32)
+    ranks = ranks.reshape(taken.shape).astype(jnp.int32)
+    each = 4
+    groups = planes * exps // each
+    offset = (lax.iota(jnp.int32, planes * exps) % each * CAP)[:, None, None]
+    spots = jnp.where(taken, ranks + offset, -1)
+    spots = spots.reshape(groups, each, local, count).transpose(0, 2, 1, 3).reshape(groups, local, each * count)
+    weights = mine.reshape(groups, each, local, count).transpose(0, 2, 1, 3).reshape(groups, local, each * count)
+    hit = spots[:, :, None, :] == lax.iota(jnp.int32, each * CAP)[None, None, :, None]
+    spread = hit.astype(jnp.bfloat16).reshape(groups, local * each * CAP, each * count)
+    slot_gates = jnp.sum(jnp.where(hit, weights[:, :, None, :], 0.0), axis=3)
+    slot_gates = slot_gates.transpose(1, 0, 2).reshape(local, groups * each * CAP, 1)
+    parts = run_experts(
+        everyone.reshape(groups, each * count, -1), spread, slot_gates, w_gate, w_up, down_weight
+    )
+    moe_out = scatter_sum(parts.reshape(planes * exps, count, width), planes, exps)
+    return mix_output(streams, mixing, post, moe_out)
+
+
 def solution(mesh):
     in_specs = (
         P(("seq", "exp"), None, None),
@@ -135,4 +523,5 @@
         P("exp", "seq", None),
     )
     out_specs = P(("seq", "exp"), None, None)
-    return jax.shard_map(body, mesh=mesh, in_specs=in_specs, out_specs=out_specs, check_vma=False)
+    chosen = fast_body if mesh.shape["exp"] == 8 else body
+    return jax.shard_map(chosen, mesh=mesh, in_specs=in_specs, out_specs=out_specs, check_vma=False)

time: 672 us -> 269 us (0.40)
  Pallas kernels: 0 us -> 230 us
  waiting for transfers between devices: 227 us -> 0 us
  blocking collectives: 220 us -> 0 us
  matrix products: 69.7 us -> 1.16 us
  local copies, waits for them, and re-layouts: 86.8 us -> 21.1 us
  other arithmetic: 48.3 us -> 16 us
  between operations: 13.8 us -> 0.36 us
    pallas_call x0 -> x3, Pallas kernels: none -> 230 us  [the longest x1 90.2 us: scatter_sum(): pl.pallas_call(functools.partial(scatter_kernel, planes, exps), out_shape...]
    all_to_all x1 -> x0, blocking collectives: 205 us -> none  [body(): lax.all_to_all(send, 'exp', split_axis=0, concat_axis=0, tiled=True)]
    all_to_all x1 -> x0, waiting for transfers between devices: 181 us -> none  [body(): lax.all_to_all(part, 'exp', split_axis=0, concat_axis=0, tiled=True)]
    dot_general x5 -> x2, matrix products: 69 us -> 0.5 us  [the longest x1 0.36 us: dense_gates(): lax.dot_general(layer_in, router, (((1,), (1,)), ((), ())), preferred_ele...]
    gather x6 -> x0, local copies, waits for them, and re-layouts: 52.1 us -> none  [the longest x1 34.7 us: weigh_slots(): jnp.take(returned_rows, targets.reshape(-1), axis=0).astype(jnp.float32)]
    reduce_scatter x1 -> x0, waiting for transfers between devices: 36.2 us -> none  [body(): lax.psum_scatter(weighted.astype(jnp.bfloat16), 'seq', scatter_dimension=...]
    reduce_sum x3 -> x1, other arithmetic: 17.5 us -> 0.65 us  [fast_body(): slot_gates = jnp.sum(jnp.where(hit, weights[:, :, None, :], 0.0), axis=3)]
    all_gather x1 -> x0, blocking collectives: 14.9 us -> none  [body(): lax.all_gather(expert_index_table, 'seq', axis=0, tiled=True)]
  transfers between devices with their start and end apart: 3 -> 0, of which waited for: 3 -> 0; matrix products, arithmetic and copies ran while one was open for 6% -> 0% of each run, Pallas kernels for 0% -> 0%
where the time goes in v1:
time: 269 us
  Pallas kernels  230 us (86%)
  local copies, waits for them, and re-layouts  21.1 us (8%)
  other arithmetic  16 us (6%)
    pallas_call x1, Pallas kernels, scatter_sum(): pl.pallas_call(functools.partial(scatter_kernel, planes, exps), out_shape...  90.2 us
    pallas_call x1, Pallas kernels, gather_tokens(): pl.pallas_call(functools.partial(gather_kernel, planes, exps), out_shape=...  72.6 us
    pallas_call x1, Pallas kernels, run_experts(): pl.pallas_call(expert_kernel, grid=(local,), out_shape=jax.ShapeDtypeStru...  67.6 us

profile of v1, /device:TPU:0, one launch (start us, length us, event | category | flops | bytes accessed | tf_op | source)
XLA Modules:
  0.0 269.0 jit_solution(16542695695212429107)
XLA Ops:
  0.0 0.9 slice.138
  0.9 3.0 %multiply_reduce_fusion = f32[64]{0:T(128)S(1)} fusion(bf16[64,4,3584]{2,1,0:T(4,128)(2,1)} %param.9), kind=kLoop, calls=%fused_computation.20 | loop fusion | flops 2752448 | bytes 1835264 | tf_op jit(solution)/shard_map/reduce_sum | solution.py:19
  3.8 0.8 fusion.113
  4.6 1.4 fusion.112
  6.1 0.7 fusion.72
  8.0 0.7 fusion.19
  8.7 1.3 fusion.89
  10.0 0.7 fusion.77
  12.2 2.7 fusion.110
  14.8 1.8 fusion.52
  17.1 0.9 concatenate.3.block
  18.0 72.6 %gather_tokens.1 = bf16[32,64,3712]{2,1,0:T(8,128)(2,1)} custom-call(bf16[64,3712]{1,0:T(8,128)(2,1)} %concatenate.3.block), custom_call_target="tpu_custom_call" | custom-call | tf_op jit(solution)/shard_map/gather_tokens/pallas_call | solution.py:232
  90.7 1.1 slice_convert_fusion
  95.3 1.7 reshape.129.slot_gates
  97.0 1.7 eq.45
  98.7 2.3 copy.73
  101.0 1.5 fusion.119.collect
  102.4 1.5 compare_convert_fusion
  103.9 2.5 copy.77.spread
  106.4 67.6 %run_experts.1 = bf16[8,256,3584]{2,1,0:T(8,128)(2,1)} custom-call(bf16[8,256,3712]{2,1,0:T(8,128)(2,1)} %bitcast.109, bf16[8,320,256]{2,1,0:T(8,128)(2,1)} %copy.77.spread, bf16[8,256,320]{2,1,0:T(8,128)(2,1)} %fusion.119.collect, f32[4,640,1]{2,1,0:T(8,128)} %reshape.129.slot_gates, bf16[4,3584,512]{2,1,0:T(8,128)(2,1)} %w_gate.1, ...), custom_call_target="tpu_custom_call" | custom-call | tf_op jit(solution)/shard_map/run_experts/pallas_call | solution.py:442
  174.1 90.2 %scatter_sum.1 = f32[64,3584]{1,0:T(8,128)S(1)} custom-call(bf16[32,64,3584]{2,1,0:T(8,128)(2,1)} %bitcast.110), custom_call_target="tpu_custom_call" | custom-call | tf_op jit(solution)/shard_map/scatter_sum/pallas_call | solution.py:348
  264.4 0.9 fusion.70
  265.3 0.9 fusion.71
  266.4 2.6 copy.79
  (67 shorter events, 6.9 us)
Async XLA Ops:
  0.0 6.9 %copy-start = (bf16[64,4,3584]{2,1,0:T(4,128)(2,1)S(1)}, bf16[64,4,3584]{2,1,0:T(4,128)(2,1)}, u32[]{:S(2)}) copy-start(bf16[64,4,3584]{2,1,0:T(4,128)(2,1)} %param.9) | copy-start | bytes 5505028
  6.9 1.1 copy-start.5
  14.8 1.8 copy-start.10
  174.0 90.3 %copy-start.1 = (bf16[64,3584]{1,0:T(8,128)(2,1)S(1)}, bf16[64,3584]{1,0:T(8,128)(2,1)}, u32[]{:S(2)}) copy-start(bf16[64,3584]{1,0:T(8,128)(2,1)} %get-tuple-element.8) | copy-start | bytes 1376260
  174.0 90.3 %copy-start.2 = (bf16[64,3584]{1,0:T(8,128)(2,1)S(1)}, bf16[64,3584]{1,0:T(8,128)(2,1)}, u32[]{:S(2)}) copy-start(bf16[64,3584]{1,0:T(8,128)(2,1)} %get-tuple-element.9) | copy-start | bytes 1376260
  174.1 90.3 %copy-start.3 = (bf16[64,3584]{1,0:T(8,128)(2,1)S(1)}, bf16[64,3584]{1,0:T(8,128)(2,1)}, u32[]{:S(2)}) copy-start(bf16[64,3584]{1,0:T(8,128)(2,1)} %get-tuple-element.10) | copy-start | bytes 1376260
  174.1 90.3 %copy-start.4 = (bf16[64,3584]{1,0:T(8,128)(2,1)S(1)}, bf16[64,3584]{1,0:T(8,128)(2,1)}, u32[]{:S(2)}) copy-start(bf16[64,3584]{1,0:T(8,128)(2,1)} %get-tuple-element.11) | copy-start | bytes 1376260
  174.1 90.3 %copy-start.6 = (f32[64]{0:T(128)S(1)}, f32[64]{0:T(128)}, u32[]{:S(2)}) copy-start(f32[64]{0:T(128)} %get-tuple-element.35) | copy-start | bytes 772
  174.1 90.3 %copy-start.7 = (f32[64]{0:T(128)S(1)}, f32[64]{0:T(128)}, u32[]{:S(2)}) copy-start(f32[64]{0:T(128)} %get-tuple-element.36) | copy-start | bytes 772
  174.1 90.3 %copy-start.8 = (f32[64]{0:T(128)S(1)}, f32[64]{0:T(128)}, u32[]{:S(2)}) copy-start(f32[64]{0:T(128)} %get-tuple-element.37) | copy-start | bytes 772
  174.1 90.3 %copy-start.9 = (f32[64]{0:T(128)S(1)}, f32[64]{0:T(128)}, u32[]{:S(2)}) copy-start(f32[64]{0:T(128)} %get-tuple-element.38) | copy-start | bytes 772

commit v2 on v1

--- a/solution.py
+++ b/solution.py
@@ -146,7 +146,8 @@
     return z, e, core, x, y, both
 
 
-def gather_kernel(planes, exps, block, out, s_z, r_z, s_1, r_1, s_2, r_2, s_c, r_c, s_own):
+def gather_kernel(planes, exps, block, pick_rank, pick_gate, want, want_across, slots, slot_gates, collect,
+                  out, staged, s_z, r_z, s_1, r_1, s_2, r_2, s_c, r_c, s_own, s_out):
     z, e, core, x, y, both = place(planes, exps)
     half_rows = block.shape[0] // 2
     first, second = (x, y), (y, x)
@@ -209,38 +210,96 @@
         for half in (0, 1):
             push(block.at[rows(half)], z, e, half, s_z.at[d - 1, half], r_z.at[d - 1, half], (lax.rem(z + d, planes), e))
     spread_own(0)
-    for k in range(1, planes + 2):
+    own.wait()
+    width = staged.shape[2]
+    room = slot_gates.shape[2]
+    each = collect.shape[1] // block.shape[0]
+    side = exps // each
+    wide = 896 if width % 896 == 0 else width
+    stores = []
+
+    def dispatch(group):
+        blocks = pl.ds(group * each, each)
+        tail = out[blocks, :, width:].reshape(collect.shape[1], 128)
+
+        def picked(left, right):
+            return lax.dot_general(left, right, (((1,), (1,)), ((), ())), preferred_element_type=jnp.float32)
+
+        hit = picked(pick_rank[...], tail) == want[...]
+        gates = jnp.sum(jnp.where(hit, picked(pick_gate[...], tail), 0.0), axis=1, keepdims=True)
+        for own_expert in range(slot_gates.shape[0]):
+            slot_gates[own_expert, group] = gates[own_expert * room : (own_expert + 1) * room]
+        spread = jnp.where(hit, 1.0, 0.0).astype(jnp.bfloat16)
+        hit_across = picked(tail, pick_rank[...]) == want_across[...]
+        collect[group] = jnp.where(hit_across, 1.0, 0.0).astype(jnp.bfloat16)
+
+        def one(i, carry):
+            columns = pl.ds(pl.multiple_of(i * wide, wide), wide)
+            rows_in = out[blocks, :, columns].reshape(collect.shape[1], wide)
+            staged[group, :, columns] = jnp.dot(spread, rows_in, preferred_element_type=jnp.float32).astype(staged.dtype)
+            return carry
+
+        lax.fori_loop(0, width // wide, one, 0)
+
+    def finish(k):
+        for half in (0, 1):
+            here = (core, swap(first[half], 1), swap(second[half], 1), swap(both, 1))
+            for index, exp in enumerate(here):
+                arrive(plane_at(k), exp, half, r_c.at[k, half, index])
+        for part in range(side):
+            group = plane_at(k) * side + part
+            dispatch(group)
+            store = pltpu.make_async_copy(staged.at[group], slots.at[group], s_out.at[k, part])
+            store.start()
+            stores.append(store)
+
+    for k in range(1, planes + 3):
         if k < planes:
             spread_own(k)
         if k - 1 < planes:
             spread_first(k - 1)
-        if k >= 2:
+        if 2 <= k < planes + 2:
             spread_second(k - 2)
-    for k in range(planes):
-        for half in (0, 1):
-            here = (core, swap(first[half], 1), swap(second[half], 1), swap(both, 1))
-            for index, exp in enumerate(here):
-                arrive(plane_at(k), exp, half, r_c.at[k, half, index])
+        if k >= 3:
+            finish(k - 3)
     for copy in started:
         copy.wait_send()
-    own.wait()
-
-
-def gather_tokens(block, planes, exps):
+    for store in stores:
+        store.wait()
+
+
+def gather_tokens(block, pick_rank, pick_gate, want, planes, exps, local):
     dma = pltpu.SemaphoreType.DMA
     shapes = [(planes - 1, 2), (planes, 2), (planes, 2, 2), (planes, 2, 4)]
+    tokens = block.shape[0]
+    width = block.shape[1] - 128
+    held, reach = want.shape
+    each = reach // tokens
+    groups = planes * exps // each
+    vmem = pl.BlockSpec(memory_space=pltpu.VMEM)
     return pl.pallas_call(
         functools.partial(gather_kernel, planes, exps),
-        out_shape=jax.ShapeDtypeStruct((planes * exps,) + block.shape, block.dtype),
-        in_specs=[pl.BlockSpec(memory_space=pl.ANY)],
-        out_specs=pl.BlockSpec(memory_space=pl.ANY),
-        scratch_shapes=[dma(shape) for shape in shapes for way in range(2)] + [dma],
-        compiler_params=pltpu.CompilerParams(collective_id=0, has_side_effects=True),
+        out_shape=[
+            jax.ShapeDtypeStruct((groups, held, width), block.dtype),
+            jax.ShapeDtypeStruct((local, groups, held // local, 1), jnp.float32),
+            jax.ShapeDtypeStruct((groups, reach, held), jnp.bfloat16),
+        ],
+        in_specs=[pl.BlockSpec(memory_space=pl.ANY)] + [vmem] * 4,
+        out_specs=[pl.BlockSpec(memory_space=pl.ANY), vmem, vmem],
+        scratch_shapes=[
+            pltpu.VMEM((planes * exps,) + block.shape, block.dtype),
+            pltpu.VMEM((groups, held, width), block.dtype),
+        ]
+        + [dma(shape) for shape in shapes for way in range(2)]
+        + [dma, dma((planes, exps // each))],
+        compiler_params=pltpu.CompilerParams(
+            collective_id=0, has_side_effects=True, vmem_limit_bytes=52 * 1024 * 1024
+        ),
         name="gather_tokens",
-    )(block)
-
-
-def scatter_kernel(planes, exps, parts, out, held, in_c, in_2, in_1, in_z,
+    )(block, pick_rank, pick_gate, want, want.T)
+
+
+def scatter_kernel(planes, exps, parts, collect, out, slots, made, in_c, in_2, in_1, in_z,
                    s_own, s_c, r_c, s_2, r_2, s_1, r_1, s_z, r_z):
     z, e, core, x, y, both = place(planes, exps)
     tokens, width = out.shape
@@ -280,56 +339,77 @@
         return (both, second[half], first[half], e)
 
     order = [k for k in range(1, planes)] + [0]
-    loads = {}
+    each = collect.shape[1] // tokens
+    side = exps // each
+    wide = 896 if width % 896 == 0 else width
+
+    def load(k, part):
+        group = plane_at(k) * side + part
+        return pltpu.make_async_copy(parts.at[group], slots.at[group], s_own.at[k, part])
+
+    def held(k, half, index):
+        return made.at[plane_at(k) * exps + dests(half)[index], rows(half)]
+
     for k in order:
+        for part in range(side):
+            load(k, part).start()
+
+    def produce(k):
+        for part in range(side):
+            load(k, part).wait()
+            group = plane_at(k) * side + part
+
+            def one(i, carry):
+                columns = pl.ds(pl.multiple_of(i * wide, wide), wide)
+                total = jnp.dot(collect[group], slots[group, :, columns], preferred_element_type=jnp.float32)
+                made[pl.ds(group * each, each), :, columns] = total.astype(made.dtype).reshape(each, tokens, wide)
+                return carry
+
+            lax.fori_loop(0, width // wide, one, 0)
         for half in (0, 1):
             for index, exp in enumerate(dests(half)):
-                away = parts.at[plane_at(k) * exps + swap(exp, 1), rows(half)]
+                away = made.at[plane_at(k) * exps + swap(exp, 1), rows(half)]
                 push(away, in_c.at[k, half, index], s_c.at[k, half, index], r_c.at[k, half, index], (z, core))
-                load = pltpu.make_async_copy(
-                    parts.at[plane_at(k) * exps + exp, rows(half)], held.at[k, half, index], s_own.at[k, half, index]
-                )
-                load.start()
-                loads[k, half, index] = load
 
     def merge_core(k):
         for half in (0, 1):
             for index in range(4):
-                loads[k, half, index].wait()
                 arrive(in_c.at[k, half, index], r_c.at[k, half, index])
-                add(held.at[k, half, index], in_c.at[k, half, index])
+                add(held(k, half, index), in_c.at[k, half, index])
                 if index < 2:
-                    push(held.at[k, half, index], in_2.at[k, half, index], s_2.at[k, half, index], r_2.at[k, half, index], (z, second[half]))
+                    push(held(k, half, index), in_2.at[k, half, index], s_2.at[k, half, index], r_2.at[k, half, index], (z, second[half]))
 
     def merge_second(k):
         for half in (0, 1):
             for index in (0, 1):
                 arrive(in_2.at[k, half, index], r_2.at[k, half, index])
-                add(held.at[k, half, 2 + index], in_2.at[k, half, index])
+                add(held(k, half, 2 + index), in_2.at[k, half, index])
                 if index == 0:
-                    push(held.at[k, half, 2], in_1.at[k, half], s_1.at[k, half], r_1.at[k, half], (z, first[half]))
+                    push(held(k, half, 2), in_1.at[k, half], s_1.at[k, half], r_1.at[k, half], (z, first[half]))
 
     def merge_first(k):
         for half in (0, 1):
             arrive(in_1.at[k, half], r_1.at[k, half])
-            add(held.at[k, half, 3], in_1.at[k, half])
+            add(held(k, half, 3), in_1.at[k, half])
             if k:
-                push(held.at[k, half, 3], in_z.at[k - 1, half], s_z.at[k - 1, half], r_z.at[k - 1, half], (plane_at(k), e))
-
-    for turn in range(planes + 2):
+                push(held(k, half, 3), in_z.at[k - 1, half], s_z.at[k - 1, half], r_z.at[k - 1, half], (plane_at(k), e))
+
+    for turn in range(planes + 3):
         if turn < planes:
-            merge_core(order[turn])
+            produce(order[turn])
         if 1 <= turn <= planes:
-            merge_second(order[turn - 1])
-        if turn >= 2:
-            merge_first(order[turn - 2])
+            merge_core(order[turn - 1])
+        if 2 <= turn <= planes + 1:
+            merge_second(order[turn - 2])
+        if turn >= 3:
+            merge_first(order[turn - 3])
     for k in range(1, planes):
         for half in (0, 1):
             arrive(in_z.at[k - 1, half], r_z.at[k - 1, half])
     for half in (0, 1):
         def one(i, carry):
             columns = pl.ds(pl.multiple_of(i * step, step), step)
-            total = held[0, half, 3, :, columns].astype(jnp.float32)
+            total = made[z * exps + e, rows(half), columns].astype(jnp.float32)
             for k in range(1, planes):
                 total = total + in_z[k - 1, half, :, columns].astype(jnp.float32)
             out[half * half_rows : (half + 1) * half_rows, columns] = total
@@ -340,124 +420,77 @@
         copy.wait_send()
 
 
-def scatter_sum(parts, planes, exps):
-    blocks, tokens, width = parts.shape
+def scatter_sum(parts, collect, planes, exps):
+    groups, held, width = parts.shape
+    tokens = collect.shape[1] * groups // (planes * exps)
     dma = pltpu.SemaphoreType.DMA
     half = (tokens // 2, width)
     shapes = [(planes, 2, 4), (planes, 2, 2), (planes, 2), (planes - 1, 2)]
+    vmem = pl.BlockSpec(memory_space=pltpu.VMEM)
     return pl.pallas_call(
         functools.partial(scatter_kernel, planes, exps),
         out_shape=jax.ShapeDtypeStruct((tokens, width), jnp.float32),
-        in_specs=[pl.BlockSpec(memory_space=pl.ANY)],
-        out_specs=pl.BlockSpec(memory_space=pltpu.VMEM),
-        scratch_shapes=[pltpu.VMEM(shape + half, parts.dtype) for shape in [shapes[0]] + shapes]
-        + [dma(shapes[0])]
+        in_specs=[pl.BlockSpec(memory_space=pl.ANY), vmem],
+        out_specs=vmem,
+        scratch_shapes=[
+            pltpu.VMEM(parts.shape, parts.dtype),
+            pltpu.VMEM((planes * exps, tokens, width), parts.dtype),
+        ]
+        + [pltpu.VMEM(shape + half, parts.dtype) for shape in shapes]
+        + [dma((planes, groups // planes))]
         + [dma(shape) for shape in shapes for way in range(2)],
         compiler_params=pltpu.CompilerParams(
-            collective_id=1, has_side_effects=True, vmem_limit_bytes=48 * 1024 * 1024
+            collective_id=1, has_side_effects=True, vmem_limit_bytes=58 * 1024 * 1024
         ),
         name="scatter_sum",
-    )(parts)
-
-
-def expert_kernel(tokens, spread, collect, slot_gates, w_gate, w_up, w_down, out,
-                  held, slots, hidden, in_sems, out_sems):
-    groups, group_rows, width = held.shape
-    own = pl.program_id(0)
-    last = pl.num_programs(0) - 1
-    room = slots.shape[1] // pl.num_programs(0)
+    )(parts, collect)
+
+
+def expert_kernel(slots, slot_gates, w_gate, w_up, w_down, out, hidden):
+    groups, room, width = slots.shape
     ff = hidden.shape[1]
     wide = 896 if width % 896 == 0 else width
     tall = 256 if ff % 256 == 0 else ff
-
-    def load(g):
-        return pltpu.make_async_copy(tokens.at[g, :, pl.ds(0, width)], held.at[g], in_sems.at[g])
-
-    def store(g):
-        return pltpu.make_async_copy(held.at[g], out.at[g], out_sems.at[g])
-
-    @pl.when(own == 0)
-    def dispatch():
-        for g in range(groups):
-            load(g).start()
-        for g in range(groups):
-            load(g).wait()
-
-            def one(i, carry):
-                columns = pl.ds(pl.multiple_of(i * wide, wide), wide)
-                slots[g, :, columns] = jnp.dot(
-                    spread[g], held[g, :, columns], preferred_element_type=jnp.float32
-                ).astype(slots.dtype)
-                return carry
-
-            lax.fori_loop(0, width // wide, one, 0)
-
-    mine = pl.ds(pl.multiple_of(own * room, room), room)
+    gates = slot_gates[0].reshape(groups * room, 1)
     for i in range(ff // tall):
         columns = pl.ds(i * tall, tall)
-        rows = slots[:, mine, :].reshape(groups * room, width)
+        rows = slots[...].reshape(groups * room, width)
         gate_part = jnp.dot(rows, w_gate[0, :, columns], preferred_element_type=jnp.float32)
         up_part = jnp.dot(rows, w_up[0, :, columns], preferred_element_type=jnp.float32)
         hidden[:, columns] = (
-            gate_part / (1.0 + jnp.exp(-gate_part)) * up_part * slot_gates[0]
+            gate_part / (1.0 + jnp.exp(-gate_part)) * up_part * gates
         ).astype(hidden.dtype)
 
     def down(i, carry):
         columns = pl.ds(pl.multiple_of(i * wide, wide), wide)
         part = jnp.dot(hidden[...], w_down[0, :, columns], preferred_element_type=jnp.float32)
-        slots[:, mine, columns] = part.astype(slots.dtype).reshape(groups, room, wide)
+        out[:, :, columns] = part.astype(out.dtype).reshape(groups, room, wide)
         return carry
 
     lax.fori_loop(0, width // wide, down, 0)
 
-    @pl.when(own == last)
-    def combine():
-        for g in range(groups):
-
-            def one(i, carry):
-                columns = pl.ds(pl.multiple_of(i * wide, wide), wide)
-                held[g, :, columns] = jnp.dot(
-                    collect[g], slots[g, :, columns], preferred_element_type=jnp.float32
-                ).astype(held.dtype)
-                return carry
-
-            lax.fori_loop(0, width // wide, one, 0)
-            store(g).start()
-        for g in range(groups):
-            store(g).wait()
-
-
-def run_experts(tokens, spread, slot_gates, w_gate, w_up, down_weight):
-    groups, rows, _ = tokens.shape
-    local, width, ff = w_gate.shape
-    room = spread.shape[1] // local
-    collect = spread.transpose(0, 2, 1)
-
-    def whole(array):
-        return pl.BlockSpec(array.shape, lambda i: (0,) * array.ndim, pipeline_mode=pl.Buffered(1))
+
+def run_experts(slots, slot_gates, w_gate, w_up, down_weight):
+    groups, held, width = slots.shape
+    local, _, ff = w_gate.shape
+    room = held // local
+    rows = pl.BlockSpec((groups, room, width), lambda i: (0, i, 0))
 
     def each(array):
-        return pl.BlockSpec((1,) + array.shape[1:], lambda i: (i, 0, 0))
+        return pl.BlockSpec((1,) + array.shape[1:], lambda i: (i,) + (0,) * (array.ndim - 1))
 
     return pl.pallas_call(
         expert_kernel,
         grid=(local,),
-        out_shape=jax.ShapeDtypeStruct((groups, rows, width), jnp.bfloat16),
-        in_specs=[pl.BlockSpec(memory_space=pl.ANY), whole(spread), whole(collect)]
-        + [each(a) for a in (slot_gates, w_gate, w_up, down_weight)],
-        out_specs=pl.BlockSpec(memory_space=pl.ANY),
-        scratch_shapes=[
-            pltpu.VMEM((groups, rows, width), jnp.bfloat16),
-            pltpu.VMEM((groups, local * room, width), jnp.bfloat16),
-            pltpu.VMEM((groups * room, ff), jnp.bfloat16),
-            pltpu.SemaphoreType.DMA((groups,)),
-            pltpu.SemaphoreType.DMA((groups,)),
-        ],
+        out_shape=jax.ShapeDtypeStruct(slots.shape, jnp.bfloat16),
+        in_specs=[rows] + [each(a) for a in (slot_gates, w_gate, w_up, down_weight)],
+        out_specs=rows,
+        scratch_shapes=[pltpu.VMEM((groups * room, ff), jnp.bfloat16)],
         compiler_params=pltpu.CompilerParams(
-            dimension_semantics=("arbitrary",), vmem_limit_bytes=64 * 1024 * 1024 - 128 * 1024
+            dimension_semantics=("arbitrary",), vmem_limit_bytes=60 * 1024 * 1024
         ),
         name="run_experts",
-    )(tokens, spread, collect, slot_gates, w_gate, w_up, down_weight)
+    )(slots, slot_gates, w_gate, w_up, down_weight)
 
 
 def dense_gates(layer_in, router, expert_index_table):
@@ -467,7 +500,11 @@
     names = lax.iota(jnp.int32, EXPERTS)
     hits = jnp.any(expert_index_table[:, :, None] == names[None, None, :], axis=1)
     chosen = jnp.where(hits, jax.nn.sigmoid(logits), 0.0)
-    return 2.5 * chosen / jnp.sum(chosen, axis=1, keepdims=True)
+    count = hits.shape[0]
+    before = (lax.iota(jnp.int32, count)[:, None] > lax.iota(jnp.int32, count)[None, :]).astype(jnp.bfloat16)
+    ranks = jnp.dot(before, hits.astype(jnp.bfloat16), preferred_element_type=jnp.float32) + 1.0
+    gates = 2.5 * chosen / jnp.sum(chosen, axis=1, keepdims=True)
+    return gates, jnp.where(hits, ranks, 0.0).astype(jnp.bfloat16)
 
 
 def fast_body(
@@ -478,35 +515,23 @@
     layer_in = mix_input(streams, pre)
     count, width = layer_in.shape
     local = w_gate.shape[0]
-    gates = dense_gates(layer_in, router, expert_index_table)
+    gates, ranks = dense_gates(layer_in, router, expert_index_table)
     high = gates.astype(jnp.bfloat16)
     low = (gates - high.astype(jnp.float32)).astype(jnp.bfloat16)
-    filler = jnp.zeros((count, 128 - 2 * EXPERTS), jnp.bfloat16)
-    block = jnp.concatenate([layer_in, high, low, filler], axis=1)
-    everyone = gather_tokens(block, planes, exps)
-    owner = lax.axis_index("exp")
-    tail = everyone[:, :, width:].astype(jnp.float32)
-    tail = tail[:, :, :EXPERTS] + tail[:, :, EXPERTS : 2 * EXPERTS]
-    mine = lax.dynamic_slice_in_dim(tail, owner * local, local, axis=2)
-    mine = mine.transpose(0, 2, 1)
-    taken = mine > 0
-    before = (lax.iota(jnp.int32, count)[:, None] < lax.iota(jnp.int32, count)[None, :]).astype(jnp.bfloat16)
-    ranks = jnp.dot(taken.astype(jnp.bfloat16).reshape(-1, count), before, preferred_element_type=jnp.float32)
-    ranks = ranks.reshape(taken.shape).astype(jnp.int32)
+    filler = jnp.zeros((count, 128 - 3 * EXPERTS), jnp.bfloat16)
+    block = jnp.concatenate([layer_in, high, low, ranks, filler], axis=1)
     each = 4
-    groups = planes * exps // each
-    offset = (lax.iota(jnp.int32, planes * exps) % each * CAP)[:, None, None]
-    spots = jnp.where(taken, ranks + offset, -1)
-    spots = spots.reshape(groups, each, local, count).transpose(0, 2, 1, 3).reshape(groups, local, each * count)
-    weights = mine.reshape(groups, each, local, count).transpose(0, 2, 1, 3).reshape(groups, local, each * count)
-    hit = spots[:, :, None, :] == lax.iota(jnp.int32, each * CAP)[None, None, :, None]
-    spread = hit.astype(jnp.bfloat16).reshape(groups, local * each * CAP, each * count)
-    slot_gates = jnp.sum(jnp.where(hit, weights[:, :, None, :], 0.0), axis=3)
-    slot_gates = slot_gates.transpose(1, 0, 2).reshape(local, groups * each * CAP, 1)
-    parts = run_experts(
-        everyone.reshape(groups, each * count, -1), spread, slot_gates, w_gate, w_up, down_weight
-    )
-    moe_out = scatter_sum(parts.reshape(planes * exps, count, width), planes, exps)
+    room = each * CAP
+    named = lax.axis_index("exp") * local + lax.iota(jnp.int32, local * room) // room
+    column = lax.iota(jnp.int32, 128)[None, :]
+    pick_gate = ((column == named[:, None]) | (column == named[:, None] + EXPERTS)).astype(jnp.bfloat16)
+    pick_rank = (column == named[:, None] + 2 * EXPERTS).astype(jnp.bfloat16)
+    spot = lax.iota(jnp.int32, local * room) % room
+    source = lax.iota(jnp.int32, each * count) // count
+    want = jnp.where(spot[:, None] // CAP == source[None, :], spot[:, None] % CAP + 1, -1).astype(jnp.float32)
+    slots, slot_gates, collect = gather_tokens(block, pick_rank, pick_gate, want, planes, exps, local)
+    parts = run_experts(slots, slot_gates, w_gate, w_up, down_weight)
+    moe_out = scatter_sum(parts, collect, planes, exps)
     return mix_output(streams, mixing, post, moe_out)
 
 

time: 269 us -> 237 us (0.88)
  local copies, waits for them, and re-layouts: 21.1 us -> 7.77 us
  Pallas kernels: 230 us -> 217 us
  other arithmetic: 16 us -> 11.2 us
    pallas_call x1, Pallas kernels: 67.6 us -> 41.2 us  [run_experts(): pl.pallas_call(expert_kernel, grid=(local,), out_shape=jax.ShapeDtypeStru...]
    pallas_call x1, Pallas kernels: 72.6 us -> 80.8 us  [gather_tokens(): pl.pallas_call(functools.partial(gather_kernel, planes, exps), out_shape=...]
    pallas_call x1, Pallas kernels: 90.2 us -> 94.6 us  [scatter_sum(): pl.pallas_call(functools.partial(scatter_kernel, planes, exps), out_shape...]
    eq x5 -> x0, local copies, waits for them, and re-layouts: 4.37 us -> none  [fast_body(): spots[:, :, None, :] == lax.iota(jnp.int32, each * CAP)[None, None, :, None]]
where the time goes in v2:
time: 237 us
  Pallas kernels  217 us (92%)
  other arithmetic  11.2 us (5%)
  local copies, waits for them, and re-layouts  7.77 us (3%)
    pallas_call x1, Pallas kernels, scatter_sum(): pl.pallas_call(functools.partial(scatter_kernel, planes, exps), out_shape...  94.6 us
    pallas_call x1, Pallas kernels, gather_tokens(): pl.pallas_call(functools.partial(gather_kernel, planes, exps), out_shape=...  80.8 us
    pallas_call x1, Pallas kernels, run_experts(): pl.pallas_call(expert_kernel, grid=(local,), out_shape=jax.ShapeDtypeStru...  41.2 us

profile of v2, /device:TPU:0, one launch (start us, length us, event | category | flops | bytes accessed | tf_op | source)
XLA Modules:
  0.0 237.0 jit_solution(14754753686067303041)
XLA Ops:
  0.0 0.9 slice.129
  0.9 3.0 %multiply_reduce_fusion = f32[64]{0:T(128)S(1)} fusion(bf16[64,4,3584]{2,1,0:T(4,128)(2,1)} %param.9), kind=kLoop, calls=%fused_computation.20 | loop fusion | flops 2752448 | bytes 1835264 | tf_op jit(solution)/shard_map/reduce_sum | solution.py:19
  4.0 0.6 fusion.122
  4.7 0.1 fusion.26
  4.9 0.2 fusion.76.pick_gate
  5.0 0.1 fusion.74.pick_rank
  5.1 0.1 select_convert_fusion.1.want
  5.3 0.1 select_convert_fusion.want_across
  5.4 0.5 copy.33
  5.9 0.7 fusion.19
  6.6 1.3 fusion.98
  7.9 0.7 fusion.79
  9.5 2.9 %fusion.121 = (bf16[64,1,3584]{2,1,0:T(2,128)(2,1)S(1)}, bf16[64,1,3584]{2,1,0:T(2,128)(2,1)S(1)}, bf16[64,1,3584]{2,1,0:T(2,128)(2,1)S(1)}, bf16[64,1,3584]{2,1,0:T(2,128)(2,1)S(1)}) fusion(bf16[64,4,3584]{2,1,0:T(4,128)(2,1)S(1)} %copy-done.2), kind=kLoop, calls=%fused_computation.241 | loop fusion | bytes 3670016 | tf_op jit(solution)/shard_map/slice | solution.py:46
  12.4 1.4 fusion.54
  13.8 0.4 fusion.124
  14.1 0.1 subtract_convert_fusion
  14.3 0.1 concatenate.3.block
  14.4 80.8 %gather_tokens.1 = (bf16[8,320,3584]{2,1,0:T(8,128)(2,1)}, f32[4,8,80,1]{3,2,1,0:T(8,128)}, bf16[8,256,320]{2,1,0:T(8,128)(2,1)}) custom-call(bf16[64,3712]{1,0:T(8,128)(2,1)S(1)} %concatenate.3.block, bf16[320,128]{1,0:T(8,128)(2,1)S(1)} %fusion.74.pick_rank, bf16[320,128]{1,0:T(8,128)(2,1)S(1)} %fusion.76.pick_gate, ...), custom_call_target="tpu_custom_call" | custom-call | tf_op jit(solution)/shard_map/gather_tokens/pallas_call | solution.py:280
  95.2 41.2 %run_experts.1.parts = bf16[8,320,3584]{2,1,0:T(8,128)(2,1)} custom-call(bf16[8,320,3584]{2,1,0:T(8,128)(2,1)} %get-tuple-element.8.slots, f32[4,8,80,1]{3,2,1,0:T(8,128)} %get-tuple-element.9.slot_gates, bf16[4,3584,512]{2,1,0:T(8,128)(2,1)} %w_gate.1, bf16[4,3584,512]{2,1,0:T(8,128)(2,1)} %w_up.1, bf16[4,512,3584]{2,1,0:T(8,128)(2,1)} %w_down.1), custom_call_target="tpu_custom_call" | custom-call | tf_op jit(solution)/shard_map/run_experts/pallas_call | solution.py:482
  136.4 94.6 %scatter_sum.1 = f32[64,3584]{1,0:T(8,128)} custom-call(bf16[8,320,3584]{2,1,0:T(8,128)(2,1)} %run_experts.1.parts, bf16[8,256,320]{2,1,0:T(8,128)(2,1)} %get-tuple-element.10.collect), custom_call_target="tpu_custom_call" | custom-call | tf_op jit(solution)/shard_map/scatter_sum/pallas_call | solution.py:430
  231.1 2.1 fusion.72
  233.2 0.9 fusion.73
  234.1 0.2 pad_maximum_fusion
  234.4 2.6 %copy.26 = bf16[64,4,3584]{2,1,0:T(4,128)(2,1)} copy(bf16[64,4,3584]{2,0,1:T(8,128)(2,1)S(1)} %pad_maximum_fusion) | data formatting | bytes 3670016 | tf_op jit(solution)/shard_map/stack | solution.py:52
  (52 shorter events, 1.1 us)
Async XLA Ops:
  0.0 5.9 %copy-start = (bf16[24,14336]{1,0:T(8,128)(2,1)S(1)}, bf16[24,14336]{1,0:T(8,128)(2,1)}, u32[]{:S(2)}) copy-start(bf16[24,14336]{1,0:T(8,128)(2,1)} %param.10) | copy-start | bytes 2064388
  0.0 5.4 %copy-start.2 = (bf16[64,4,3584]{2,1,0:T(4,128)(2,1)S(1)}, bf16[64,4,3584]{2,1,0:T(4,128)(2,1)}, u32[]{:S(2)}) copy-start(bf16[64,4,3584]{2,1,0:T(4,128)(2,1)} %param.9) | copy-start | bytes 5505028
  0.0 3.9 %copy-start.7 = (f32[24]{0:T(128)S(1)}, f32[24]{0:T(128)}, u32[]{:S(2)}) copy-start(f32[24]{0:T(128)} %param.12) | copy-start | bytes 292
  0.0 4.6 %copy-start.6 = (s32[64,8]{0,1:T(8,128)S(1)}, s32[64,8]{0,1:T(8,128)}, u32[]{:S(2)}) copy-start(s32[64,8]{0,1:T(8,128)} %param.14) | copy-start | bytes 6148
  0.0 3.9 %copy-start.5 = (f32[3]{0:T(128)S(1)}, f32[3]{0:T(128)}, u32[]{:S(2)}) copy-start(f32[3]{0:T(128)} %param.11) | copy-start | bytes 40
  12.4 1.4 copy-start.8
  136.4 94.6 %copy-start.4 = (bf16[64,3584]{1,0:T(8,128)(2,1)S(1)}, bf16[64,3584]{1,0:T(8,128)(2,1)}, u32[]{:S(2)}) copy-start(bf16[64,3584]{1,0:T(8,128)(2,1)} %get-tuple-element.15) | copy-start | bytes 1376260
  231.1 2.2 copy-start.3
  234.1 2.9 %copy-start.1 = (bf16[24,14336]{1,0:T(8,128)(2,1)S(1)}, bf16[24,14336]{1,0:T(8,128)(2,1)}, u32[]{:S(2)}) copy-start(bf16[24,14336]{1,0:T(8,128)(2,1)} %param.10) | copy-start | bytes 2064388

commit v3 on v2

--- a/solution.py
+++ b/solution.py
@@ -132,6 +132,15 @@
     return exp + bit - 2 * bit * side
 
 
+def partner(plane, k):
+    bit = 1
+    while bit <= k:
+        if k & bit:
+            plane = swap(plane, bit)
+        bit *= 2
+    return plane
+
+
 def greet(peers):
     barrier = pltpu.get_barrier_semaphore()
     for peer in peers:
@@ -151,7 +160,7 @@
     z, e, core, x, y, both = place(planes, exps)
     half_rows = block.shape[0] // 2
     first, second = (x, y), (y, x)
-    greet([(lax.rem(z + d, planes), e) for d in range(1, planes)] + [(z, x), (z, y), (z, core)])
+    greet([(partner(z, d), e) for d in range(1, planes)] + [(z, x), (z, y), (z, core)])
     started = []
 
     def rows(half):
@@ -174,7 +183,7 @@
         pltpu.make_async_copy(spot, spot, sem).wait()
 
     def plane_at(k):
-        return lax.rem(z + planes - k, planes)
+        return partner(z, k)
 
     def local(k, exp, half):
         if k == 0 and exp is e:
@@ -208,7 +217,7 @@
     own.start()
     for d in range(1, planes):
         for half in (0, 1):
-            push(block.at[rows(half)], z, e, half, s_z.at[d - 1, half], r_z.at[d - 1, half], (lax.rem(z + d, planes), e))
+            push(block.at[rows(half)], z, e, half, s_z.at[d - 1, half], r_z.at[d - 1, half], (partner(z, d), e))
     spread_own(0)
     own.wait()
     width = staged.shape[2]
@@ -254,10 +263,10 @@
             stores.append(store)
 
     for k in range(1, planes + 3):
+        if k - 1 < planes:
+            spread_first(k - 1)
         if k < planes:
             spread_own(k)
-        if k - 1 < planes:
-            spread_first(k - 1)
         if 2 <= k < planes + 2:
             spread_second(k - 2)
         if k >= 3:
@@ -306,7 +315,7 @@
     half_rows = tokens // 2
     step = 512 if width % 512 == 0 else width
     first, second = (x, y), (y, x)
-    greet([(lax.rem(z + d, planes), e) for d in range(1, planes)] + [(z, x), (z, y), (z, core)])
+    greet([(partner(z, d), e) for d in range(1, planes)] + [(z, x), (z, y), (z, core)])
     started = []
 
     def rows(half):
@@ -333,12 +342,12 @@
         lax.fori_loop(0, width // step, one, 0)
 
     def plane_at(k):
-        return lax.rem(z + k, planes)
+        return partner(z, k)
 
     def dests(half):
         return (both, second[half], first[half], e)
 
-    order = [k for k in range(1, planes)] + [0]
+    order = [k for k in range(planes - 1, -1, -1)]
     each = collect.shape[1] // tokens
     side = exps // each
     wide = 896 if width % 896 == 0 else width
@@ -399,10 +408,10 @@
             produce(order[turn])
         if 1 <= turn <= planes:
             merge_core(order[turn - 1])
+        if turn >= 3:
+            merge_first(order[turn - 3])
         if 2 <= turn <= planes + 1:
             merge_second(order[turn - 2])
-        if turn >= 3:
-            merge_first(order[turn - 3])
     for k in range(1, planes):
         for half in (0, 1):
             arrive(in_z.at[k - 1, half], r_z.at[k - 1, half])
@@ -548,5 +557,5 @@
         P("exp", "seq", None),
     )
     out_specs = P(("seq", "exp"), None, None)
-    chosen = fast_body if mesh.shape["exp"] == 8 else body
+    chosen = fast_body if (mesh.shape["seq"], mesh.shape["exp"]) == (4, 8) else body
     return jax.shard_map(chosen, mesh=mesh, in_specs=in_specs, out_specs=out_specs, check_vma=False)

time: 237 us -> 232 us (0.979)
  Pallas kernels: 217 us -> 212 us
    pallas_call x1, Pallas kernels: 94.6 us -> 88.4 us  [scatter_sum(): pl.pallas_call(functools.partial(scatter_kernel, planes, exps), out_shape...]
where the time goes in v3:
time: 232 us
  Pallas kernels  212 us (91%)
  other arithmetic  11.2 us (5%)
  local copies, waits for them, and re-layouts  7.77 us (3%)
    pallas_call x1, Pallas kernels, scatter_sum(): pl.pallas_call(functools.partial(scatter_kernel, planes, exps), out_shape...  88.4 us
    pallas_call x1, Pallas kernels, gather_tokens(): pl.pallas_call(functools.partial(gather_kernel, planes, exps), out_shape=...  82.2 us
    pallas_call x1, Pallas kernels, run_experts(): pl.pallas_call(expert_kernel, grid=(local,), out_shape=jax.ShapeDtypeStru...  41.2 us

profile of v3, /device:TPU:0, one launch (start us, length us, event | category | flops | bytes accessed | tf_op | source)
XLA Modules:
  0.0 232.2 jit_solution(6718319625885608663)
XLA Ops:
  0.0 0.9 slice.129
  0.9 3.0 %multiply_reduce_fusion = f32[64]{0:T(128)S(1)} fusion(bf16[64,4,3584]{2,1,0:T(4,128)(2,1)} %param.9), kind=kLoop, calls=%fused_computation.20 | loop fusion | flops 2752448 | bytes 1835264 | tf_op jit(solution)/shard_map/reduce_sum | solution.py:19
  4.0 0.6 fusion.122
  4.7 0.1 fusion.26
  4.9 0.2 fusion.76.pick_gate
  5.0 0.1 fusion.74.pick_rank
  5.1 0.1 select_convert_fusion.1.want
  5.3 0.1 select_convert_fusion.want_across
  5.4 0.5 copy.33
  5.9 0.7 fusion.19
  6.6 1.3 fusion.98
  7.9 0.7 fusion.79
  9.5 2.9 %fusion.121 = (bf16[64,1,3584]{2,1,0:T(2,128)(2,1)S(1)}, bf16[64,1,3584]{2,1,0:T(2,128)(2,1)S(1)}, bf16[64,1,3584]{2,1,0:T(2,128)(2,1)S(1)}, bf16[64,1,3584]{2,1,0:T(2,128)(2,1)S(1)}) fusion(bf16[64,4,3584]{2,1,0:T(4,128)(2,1)S(1)} %copy-done.2), kind=kLoop, calls=%fused_computation.241 | loop fusion | bytes 3670016 | tf_op jit(solution)/shard_map/slice | solution.py:46
  12.4 1.4 fusion.54
  13.8 0.4 fusion.124
  14.1 0.1 subtract_convert_fusion
  14.3 0.1 concatenate.3.block
  14.4 82.2 %gather_tokens.1 = (bf16[8,320,3584]{2,1,0:T(8,128)(2,1)}, f32[4,8,80,1]{3,2,1,0:T(8,128)}, bf16[8,256,320]{2,1,0:T(8,128)(2,1)}) custom-call(bf16[64,3712]{1,0:T(8,128)(2,1)S(1)} %concatenate.3.block, bf16[320,128]{1,0:T(8,128)(2,1)S(1)} %fusion.74.pick_rank, bf16[320,128]{1,0:T(8,128)(2,1)S(1)} %fusion.76.pick_gate, ...), custom_call_target="tpu_custom_call" | custom-call | tf_op jit(solution)/shard_map/gather_tokens/pallas_call | solution.py:289
  96.6 41.2 %run_experts.1.parts = bf16[8,320,3584]{2,1,0:T(8,128)(2,1)} custom-call(bf16[8,320,3584]{2,1,0:T(8,128)(2,1)} %get-tuple-element.8.slots, f32[4,8,80,1]{3,2,1,0:T(8,128)} %get-tuple-element.9.slot_gates, bf16[4,3584,512]{2,1,0:T(8,128)(2,1)} %w_gate.1, bf16[4,3584,512]{2,1,0:T(8,128)(2,1)} %w_up.1, bf16[4,512,3584]{2,1,0:T(8,128)(2,1)} %w_down.1), custom_call_target="tpu_custom_call" | custom-call | tf_op jit(solution)/shard_map/run_experts/pallas_call | solution.py:491
  137.8 88.4 %scatter_sum.1 = f32[64,3584]{1,0:T(8,128)} custom-call(bf16[8,320,3584]{2,1,0:T(8,128)(2,1)} %run_experts.1.parts, bf16[8,256,320]{2,1,0:T(8,128)(2,1)} %get-tuple-element.10.collect), custom_call_target="tpu_custom_call" | custom-call | tf_op jit(solution)/shard_map/scatter_sum/pallas_call | solution.py:439
  226.2 2.1 fusion.72
  228.4 0.9 fusion.73
  229.3 0.2 pad_maximum_fusion
  229.6 2.6 %copy.26 = bf16[64,4,3584]{2,1,0:T(4,128)(2,1)} copy(bf16[64,4,3584]{2,0,1:T(8,128)(2,1)S(1)} %pad_maximum_fusion) | data formatting | bytes 3670016 | tf_op jit(solution)/shard_map/stack | solution.py:52
  (52 shorter events, 1.1 us)
Async XLA Ops:
  0.0 5.9 %copy-start = (bf16[24,14336]{1,0:T(8,128)(2,1)S(1)}, bf16[24,14336]{1,0:T(8,128)(2,1)}, u32[]{:S(2)}) copy-start(bf16[24,14336]{1,0:T(8,128)(2,1)} %param.10) | copy-start | bytes 2064388
  0.0 5.4 %copy-start.2 = (bf16[64,4,3584]{2,1,0:T(4,128)(2,1)S(1)}, bf16[64,4,3584]{2,1,0:T(4,128)(2,1)}, u32[]{:S(2)}) copy-start(bf16[64,4,3584]{2,1,0:T(4,128)(2,1)} %param.9) | copy-start | bytes 5505028
  0.0 3.9 %copy-start.7 = (f32[24]{0:T(128)S(1)}, f32[24]{0:T(128)}, u32[]{:S(2)}) copy-start(f32[24]{0:T(128)} %param.12) | copy-start | bytes 292
  0.0 4.6 %copy-start.6 = (s32[64,8]{0,1:T(8,128)S(1)}, s32[64,8]{0,1:T(8,128)}, u32[]{:S(2)}) copy-start(s32[64,8]{0,1:T(8,128)} %param.14) | copy-start | bytes 6148
  0.0 3.9 %copy-start.5 = (f32[3]{0:T(128)S(1)}, f32[3]{0:T(128)}, u32[]{:S(2)}) copy-start(f32[3]{0:T(128)} %param.11) | copy-start | bytes 40
  12.4 1.4 copy-start.8
  137.8 88.4 %copy-start.4 = (bf16[64,3584]{1,0:T(8,128)(2,1)S(1)}, bf16[64,3584]{1,0:T(8,128)(2,1)}, u32[]{:S(2)}) copy-start(bf16[64,3584]{1,0:T(8,128)(2,1)} %get-tuple-element.15) | copy-start | bytes 1376260
  226.2 2.2 copy-start.3
  229.3 2.9 %copy-start.1 = (bf16[24,14336]{1,0:T(8,128)(2,1)S(1)}, bf16[24,14336]{1,0:T(8,128)(2,1)}, u32[]{:S(2)}) copy-start(bf16[24,14336]{1,0:T(8,128)(2,1)} %param.10) | copy-start | bytes 2064388
